TPU v7x, 512 devices: a whole 4x4x16 slice. The times are simulated.
512 devices in a mesh: row: 32 (over y, z_lo), col: 16 (over z_hi, x, core).
Axes of the slice: x: 4, y: 4, z: 16 (z_hi: 2, z_lo: 8; z = z_hi * 8 + z_lo), core: 2. Of those that a mesh axis runs over, the one named last changes fastest.
Arguments:
- amplitudes: float32 [32, 32, 384, 384], P('row', 'col'), may hold values from -6 to 6
- exchange_ints: float32 [32, 32, 384, 384], P('row', 'col'), may hold values from -6 to 6
- virt_fock: float32 [384, 384], replicated, as said below
- intersection: float32 [384, 384], replicated, as said below
- occ_fock: float32 [32, 32], replicated, may hold values from -1.5 to 0.3, as said below
- virt_energy: float32 [384], replicated, may hold values from 1 to 3
- fock_tiles: int32 [3, 3], replicated, may hold values from 0 to 1, as said below
- intersection_tiles: int32 [3, 3], replicated, may hold values from 0 to 1, as said below
- occ_pattern: int32 [32, 32], replicated, may hold values from 0 to 1, as said below
- pair_domain: int32 [32, 32, 3], P('row', 'col'), may hold values 0 or 1
Outputs:
- new_amplitudes: float32 [32, 32, 384, 384], P('row', 'col')
Inputs may be any that keep to these rules, and one draw needn't show every extreme that they name: `virt_fock`: symmetric. `intersection`: symmetric. `occ_fock`: diagonal entries between -1.5 and -0.3, the others between -0.3 and 0.3. `fock_tiles`: symmetric, every diagonal tile 1, some off-diagonal tile 0. `intersection_tiles`: symmetric, every diagonal tile 1, some off-diagonal tile 0. `occ_pattern`: 1 on the diagonal, 0 where the two orbitals lie more than 1 apart in index.
All inputs are finite; a program needn't handle non-finite values. No bound on the sum of `pair_domain` on one device may be relied on, other than what follows from the above.
Results may differ from a plain program's by a relative error of at most 0.0001.
Values sent between devices are 32-bit elements; how exact they have to be, the bound alone decides.
A program may use at most 64 MiB of HBM per device.

v0:
```python
import jax
import jax.numpy as jnp
from jax import lax
from jax.sharding import PartitionSpec as P

TILE = 128
BAND = 1
ITERS = 2


HIGHEST = lax.Precision.HIGHEST


def padded_2(cells, sides, width):
    for axis, dim in sides:
        count = lax.axis_size(axis)
        ends = count - 1
        head = lax.slice_in_dim(cells, 0, width, axis=dim)
        tail = lax.slice_in_dim(cells, cells.shape[dim] - width, cells.shape[dim], axis=dim)
        cells = jnp.concatenate(
            [
                lax.ppermute(tail, axis, [(i, (i + 1) % count) for i in range(ends)]),
                cells,
                lax.ppermute(head, axis, [((i + 1) % count, i) for i in range(ends)]),
            ],
            axis=dim,
        )
    return cells


def expand_tiles(tiles):
    return jnp.repeat(jnp.repeat(tiles.astype(jnp.float32), TILE, axis=0), TILE, axis=1)


def sandwich(left_mat, blocks, right_mat):
    partial_value = jnp.einsum("ijab,bc->ijac", blocks, right_mat, precision=HIGHEST)
    return jnp.einsum("ac,ijcb->ijab", left_mat, partial_value, precision=HIGHEST)


def mirror_blocks(blocks):
    section_one = lax.all_to_all(blocks, "col", split_axis=2, concat_axis=1, tiled=True)
    section_two = lax.all_to_all(section_one, "row", split_axis=1, concat_axis=0, tiled=True)
    section_three = lax.all_to_all(section_two, "col", split_axis=0, concat_axis=2, tiled=True)
    return jnp.transpose(section_three, (1, 0, 3, 2))


def shards(
    amplitudes,
    exchange_ints,
    virt_fock,
    intersection,
    occ_fock,
    virt_energy,
    fock_tiles,
    intersection_tiles,
    occ_pattern,
    pair_domain,
):
    rows_dev = amplitudes.shape[0]
    cols_dev = amplitudes.shape[1]
    fock_eff = virt_fock * expand_tiles(fock_tiles)
    over_eff = intersection * expand_tiles(intersection_tiles)
    coupling = occ_fock * occ_pattern.astype(jnp.float32)
    padded = jnp.pad(coupling, ((0, 0), (BAND, BAND)))
    row_start = lax.axis_index("row") * rows_dev
    col_start = lax.axis_index("col") * cols_dev
    row_coup = lax.dynamic_slice(padded, (row_start, row_start), (rows_dev, rows_dev + 2 * BAND))
    occ_diag = jnp.diagonal(occ_fock)
    occ_rows = lax.dynamic_slice_in_dim(occ_diag, row_start, rows_dev)
    occ_cols = lax.dynamic_slice_in_dim(occ_diag, col_start, cols_dev)
    denominator = (
        virt_energy[None, None, :, None]
        + virt_energy[None, None, None, :]
        - occ_rows[:, None, None, None]
        - occ_cols[None, :, None, None]
    )
    domain = jnp.repeat(pair_domain.astype(jnp.float32), TILE, axis=2)
    step_scale = domain[:, :, :, None] * domain[:, :, None, :] / denominator
    current = amplitudes
    for iteration in range(ITERS):
        nearby = padded_2(current, (("row", 0),), BAND)
        coupled = jnp.einsum("ik,kjab->ijab", row_coup, nearby, precision=HIGHEST)
        half_resid = sandwich(fock_eff, current, over_eff) - sandwich(over_eff, coupled, over_eff)
        mirrored = mirror_blocks(half_resid)
        residual = exchange_ints + half_resid + mirrored
        current = current - step_scale * residual
    return current


def solution(mesh):
    in_specs = (
        P("row", "col", None, None),
        P("row", "col", None, None),
        P(),
        P(),
        P(),
        P(),
        P(),
        P(),
        P(),
        P("row", "col", None),
    )
    out_specs = P("row", "col", None, None)
    return jax.shard_map(shards, mesh=mesh, in_specs=in_specs, out_specs=out_specs, check_vma=False)
```

profile of v0, /device:TPU:33, one launch (start us, length us, event | category | flops | bytes accessed | tf_op | source)
XLA Modules:
  0.0 578.8 jit_solution(18274720167475628434)
XLA Ops:
  0.0 3.7 collective-permute-start
  3.7 2.7 collective-permute-start.1
  9.7 2.1 convolution_bitcast_fusion
  11.7 2.4 fusion.19
  14.2 14.4 %collective-permute-done = f32[1,2,384,384]{3,2,1,0:T(8,128)} collective-permute-done((f32[1,2,384,384]{3,2,1,0:T(8,128)}, f32[1,2,384,384]{3,2,1,0:T(8,128)}, u32[]{:S(2)}, u32[]{:S(2)}) %collective-permute-start) | collective-permute-done | bytes 1179680 | tf_op jit(solution)/shard_map/ppermute | solution.py:22
  28.6 29.5 %collective-permute-done.1 = f32[1,2,384,384]{3,2,1,0:T(8,128)} collective-permute-done((f32[1,2,384,384]{3,2,1,0:T(8,128)}, f32[1,2,384,384]{3,2,1,0:T(8,128)}, u32[]{:S(2)}, u32[]{:S(2)}) %collective-permute-start.1) | collective-permute-done | bytes 1179680 | tf_op jit(solution)/shard_map/ppermute | solution.py:24
  58.1 1.9 pad_maximum_fusion
  60.0 10.4 %fusion = f32[1,2,384,384]{3,0,2,1:T(1,128)S(1)} fusion(f32[3,2,384,384]{3,2,1,0:T(8,128)S(1)} %pad_maximum_fusion, s32[]{:T(128)S(6)} %select_n.14, s32[]{:T(128)S(6)} %select_n.16, f32[32,32]{1,0:T(8,128)S(1)} %convert_multiply_fusion), kind=kOutput, calls=%fused_computation.1 | convolution fusion | flops 10616832 | bytes 4722696 | tf_op jit(solution)/shard_map/ik,kjab->ijab/dot_general | solution.py:82
  70.4 2.1 fusion.12
  72.4 2.4 fusion.2
  74.8 2.0 copy.42
  76.9 81.3 %all_to_all.96 = f32[1,2,384,384]{3,1,0,2:T(2,128)S(1)} all-to-all(f32[1,2,384,384]{3,1,0,2:T(2,128)} %copy.42), channel_id=1, replica_groups=mesh['row'=32,'col'=16] {'col'}, dimensions={2} | all-to-all | bytes 2359296 | tf_op jit(solution)/shard_map/all_to_all | solution.py:41
  158.3 66.1 %all_to_all.97 = f32[1,32,24,384]{3,2,0,1:T(8,128)} all-to-all(f32[1,32,24,384]{3,2,0,1:T(8,128)S(1)} %bitcast.133), channel_id=1, replica_groups=mesh['row'=32,'col'=16] {'row'}, dimensions={1} | all-to-all | bytes 2359296 | tf_op jit(solution)/shard_map/all_to_all | solution.py:42
  224.4 5.0 all-to-all-start.2
  235.2 1.7 add_subtract_fusion
  236.8 56.6 %all-to-all-done.2 = f32[32,1,24,384]{3,2,1,0:T(8,128)S(1)} async-done(((f32[32,1,24,384]{3,2,1,0:T(8,128)}), f32[32,1,24,384]{3,2,1,0:T(8,128)S(1)}, u32[]{:S(2)}, u32[]{:S(2)}) %all-to-all-start.2) | async-done | bytes 1179680 | tf_op jit(solution)/shard_map/all_to_all | solution.py:43
  294.9 1.7 fusion.7
  296.6 1.9 collective-permute-start.2
  298.5 3.4 collective-permute-start.3
  302.0 2.1 fusion.10
  304.1 3.3 fusion.17
  307.4 18.1 %collective-permute-done.2 = f32[1,2,384,384]{2,3,1,0:T(8,128)S(1)} collective-permute-done((f32[1,2,384,384]{2,3,1,0:T(8,128)S(1)}, f32[1,2,384,384]{2,3,1,0:T(8,128)S(1)}, u32[]{:S(2)}, u32[]{:S(2)}) %collective-permute-start.2) | collective-permute-done | bytes 1179680 | tf_op jit(solution)/shard_map/ppermute | solution.py:22
  325.5 16.5 %collective-permute-done.3 = f32[1,2,384,384]{2,3,1,0:T(8,128)S(1)} collective-permute-done((f32[1,2,384,384]{2,3,1,0:T(8,128)S(1)}, f32[1,2,384,384]{2,3,1,0:T(8,128)S(1)}, u32[]{:S(2)}, u32[]{:S(2)}) %collective-permute-start.3) | collective-permute-done | bytes 1179680 | tf_op jit(solution)/shard_map/ppermute | solution.py:24
  342.0 2.1 pad_maximum_fusion.1
  344.1 6.3 %copy.76 = f32[3,2,384,384]{3,0,2,1:T(4,128)} copy(f32[3,2,384,384]{2,3,1,0:T(8,128)} %pad_maximum_fusion.1) | data formatting | bytes 7077888 | tf_op jit(solution)/shard_map/concatenate | solution.py:20
  350.4 10.4 %fusion.27 = f32[1,2,384,384]{3,0,2,1:T(1,128)S(1)} fusion(f32[3,2,384,384]{3,0,2,1:T(4,128)} %copy.76, s32[]{:T(128)S(6)} %select_n.14, s32[]{:T(128)S(6)} %select_n.16, f32[32,32]{1,0:T(8,128)S(1)} %copy-done.10), kind=kOutput, calls=%fused_computation.48 | convolution fusion | flops 10616832 | bytes 4722696 | tf_op jit(solution)/shard_map/ik,kjab->ijab/dot_general | solution.py:82
  360.8 2.1 fusion.8
  362.9 3.3 fusion.3
  366.2 2.4 copy.57
  368.7 56.6 %all_to_all.98 = f32[1,2,384,384]{3,1,0,2:T(2,128)S(1)} all-to-all(f32[1,2,384,384]{3,1,0,2:T(2,128)S(1)} %copy.57), channel_id=1, replica_groups=mesh['row'=32,'col'=16] {'col'}, dimensions={2} | all-to-all | bytes 2359296 | tf_op jit(solution)/shard_map/all_to_all | solution.py:41
  425.4 73.2 %all_to_all.99 = f32[1,32,24,384]{3,2,0,1:T(8,128)S(1)} all-to-all(f32[1,32,24,384]{3,2,0,1:T(8,128)S(1)} %bitcast.135), channel_id=1, replica_groups=mesh['row'=32,'col'=16] {'row'}, dimensions={1} | all-to-all | bytes 2359296 | tf_op jit(solution)/shard_map/all_to_all | solution.py:42
  498.6 76.9 %all_to_all.100 = f32[32,1,24,384]{3,2,1,0:T(8,128)S(1)} all-to-all(f32[32,1,24,384]{3,2,1,0:T(8,128)S(1)} %bitcast.136), channel_id=1, replica_groups=mesh['row'=32,'col'=16] {'col'}, dimensions={0} | all-to-all | bytes 2359296 | tf_op jit(solution)/shard_map/all_to_all | solution.py:43
  (70 shorter events, 13.9 us)
Async XLA Ops:
  0.0 7.7 %copy-start.17 = (s32[3,3]{1,0:T(4,128)S(1)}, s32[3,3]{1,0:T(4,128)}, u32[]{:S(2)}) copy-start(s32[3,3]{1,0:T(4,128)} %param.17) | copy-start | bytes 112
  0.0 7.9 %copy-start.8 = (f32[384,384]{1,0:T(8,128)S(1)}, f32[384,384]{1,0:T(8,128)}, u32[]{:S(2)}) copy-start(f32[384,384]{1,0:T(8,128)} %param.12) | copy-start | bytes 1769476
  0.0 28.6 %collective-permute-start = (f32[1,2,384,384]{3,2,1,0:T(8,128)}, f32[1,2,384,384]{3,2,1,0:T(8,128)}, u32[]{:S(2)}, u32[]{:S(2)}) collective-permute-start(f32[1,2,384,384]{3,2,1,0:T(8,128)} %param.10), channel_id=1, source_target_pairs={{0,16},{16,32},{32,48},{48,64},{64,80},{80,96},{96,112},{112,128},... | collective-permute-start | bytes 3538952 | tf_op jit(solution)/shard_map/ppermute | solution.py:22
  3.7 54.4 %collective-permute-start.1 = (f32[1,2,384,384]{3,2,1,0:T(8,128)}, f32[1,2,384,384]{3,2,1,0:T(8,128)}, u32[]{:S(2)}, u32[]{:S(2)}) collective-permute-start(f32[1,2,384,384]{3,2,1,0:T(8,128)} %param.10), channel_id=1, source_target_pairs={{16,0},{32,16},{48,32},{64,48},{80,64},{96,80},{112,96},{128,112},... | collective-permute-start | bytes 3538952 | tf_op jit(solution)/shard_map/ppermute | solution.py:24
  6.4 1.7 copy-start.18
  8.4 0.7 copy-start
  8.4 0.7 copy-start.13
  8.4 1.3 copy-start.1
  9.7 50.3 %copy-start.9 = (f32[32,32]{1,0:T(8,128)}, f32[32,32]{1,0:T(8,128)S(1)}, u32[]{:S(2)}) copy-start(f32[32,32]{1,0:T(8,128)S(1)} %convert_multiply_fusion) | copy-start | bytes 12292
  74.8 2.0 copy-start.2
  224.4 69.0 %all-to-all-start.2 = ((f32[32,1,24,384]{3,2,1,0:T(8,128)}), f32[32,1,24,384]{3,2,1,0:T(8,128)S(1)}, u32[]{:S(2)}, u32[]{:S(2)}) async-start(f32[32,1,24,384]{3,2,1,0:T(8,128)} %bitcast.131), calls=%async_computation.2 | async-start | bytes 2359296 | tf_op jit(solution)/shard_map/all_to_all | solution.py:43
  232.8 1.7 copy-start.19
  232.8 2.4 copy-start.14
  293.5 1.3 copy-start.3
  293.5 1.4 copy-start.5
  293.5 1.4 copy-start.11
  293.5 1.4 copy-start.15
  296.6 28.9 %collective-permute-start.2 = (f32[1,2,384,384]{2,3,1,0:T(8,128)S(1)}, f32[1,2,384,384]{2,3,1,0:T(8,128)S(1)}, u32[]{:S(2)}, u32[]{:S(2)}) collective-permute-start(f32[1,2,384,384]{2,3,1,0:T(8,128)S(1)} %fusion.7), channel_id=1, source_target_pairs={{0,16},{16,32},{32,48},{48,64},{64,80},{80,96},{96,112},{112,128},... | collective-permute-start | bytes 3538952 | tf_op jit(solution)/shard_map/ppermute | solution.py:22
  298.5 43.5 %collective-permute-start.3 = (f32[1,2,384,384]{2,3,1,0:T(8,128)S(1)}, f32[1,2,384,384]{2,3,1,0:T(8,128)S(1)}, u32[]{:S(2)}, u32[]{:S(2)}) collective-permute-start(f32[1,2,384,384]{2,3,1,0:T(8,128)S(1)} %fusion.7), channel_id=1, source_target_pairs={{16,0},{32,16},{48,32},{64,48},{80,64},{96,80},{112,96},{128,112},... | collective-permute-start | bytes 3538952 | tf_op jit(solution)/shard_map/ppermute | solution.py:24
  344.1 6.3 %copy-start.10 = (f32[32,32]{1,0:T(8,128)S(1)}, f32[32,32]{1,0:T(8,128)}, u32[]{:S(2)}) copy-start(f32[32,32]{1,0:T(8,128)} %copy-done.9) | copy-start | bytes 12292
  360.8 2.1 copy-start.7
  575.5 1.3 copy-start.4
  575.5 1.4 copy-start.6
  575.5 1.4 copy-start.12
  575.5 1.4 copy-start.16
where the time goes:
time: 580 us; the launch traced here: 579 us
  blocking collectives  354 us (61%)
  waiting for transfers between devices  135 us (23%)
  matrix products  40.5 us (7%)
  local copies, waits for them, and re-layouts  24.1 us (4%)
  starting transfers between devices  16.7 us (3%)
  other arithmetic  7.91 us (1%)
    all_to_all x2, blocking collectives, mirror_blocks(): lax.all_to_all(section_one, 'row', split_axis=1, concat_axis=0, tiled=True)  139 us
    all_to_all x2, blocking collectives, mirror_blocks(): lax.all_to_all(blocks, 'col', split_axis=2, concat_axis=1, tiled=True)  138 us
    all_to_all x1, blocking collectives, mirror_blocks(): lax.all_to_all(section_two, 'col', split_axis=0, concat_axis=2, tiled=True)  76.9 us
    all_to_all x1, waiting for transfers between devices, mirror_blocks(): lax.all_to_all(section_two, 'col', split_axis=0, concat_axis=2, tiled=True)  56.6 us
    ppermute x2, waiting for transfers between devices, padded_2(): lax.ppermute(head, axis, [((i + 1) % count, i) for i in range(ends)])  46 us
    ppermute x2, waiting for transfers between devices, padded_2(): lax.ppermute(tail, axis, [(i, (i + 1) % count) for i in range(ends)])  32.5 us
    dot_general x2, matrix products, shards(): coupled = jnp.einsum('ik,kjab->ijab', row_coup, nearby, precision=HIGHEST)  20.8 us
  transfers between devices with their start and end apart: 5, of which 5 were waited for; matrix products, arithmetic and copies ran while one was open for 3% of the time, Pallas kernels for 0%

commit v1 on v0

v1 whole, which is shorter than its diff:
```python
import functools

import jax
import jax.numpy as jnp
from jax import lax
from jax.experimental import pallas as pl
from jax.experimental.pallas import tpu as pltpu
from jax.sharding import PartitionSpec as P

TILE = 128
NT = 3
NV = 384
NCH = 3
CH = NV // NCH
ITERS = 2
MESH = pl.DeviceIdType.MESH
HIGHEST = lax.Precision.HIGHEST


def bit(value, place):
    return (value // (1 << place)) % 2


def xor(*bits):
    total = bits[0]
    for one in bits[1:]:
        total = total + one
    return total % 2


def dot_nt(left, right):
    return lax.dot_general(left, right, (((1,), (1,)), ((), ())), precision=HIGHEST, preferred_element_type=jnp.float32)


def dot_nn(left, right):
    return lax.dot_general(left, right, (((1,), (0,)), ((), ())), precision=HIGHEST, preferred_element_type=jnp.float32)


def kernel(
    x_ref, k_ref, fock_ref, over_ref, occ_ref, ener_ref, ftile_ref, otile_ref, opat_ref, dom_ref,
    out_ref,
    fe, se, mm, x1, hbuf, rbuf, mbuf, gt, dd, gg, scale, ener, vtw,
    hs, hr, l1s, l1r, l2s, l2r,
):
    row = lax.axis_index("row")
    col = lax.axis_index("col")
    y1, y0, a2, a1, a0 = (bit(row, n) for n in (4, 3, 2, 1, 0))
    zh, x1b, x0, core = (bit(col, n) for n in (3, 2, 1, 0))

    def at(y1_, y0_, a2_, a1_, a0_, zh_, x1_, x0_, core_):
        return y1_ * 16 + y0_ * 8 + a2_ * 4 + a1_ * 2 + a0_, zh_ * 8 + x1_ * 4 + x0_ * 2 + core_

    def other(device):
        return jnp.logical_or(device[0] != row, device[1] != col)

    def relay_of(s):
        return at(xor(core, a1), y0, a2, a1, a0, zh, x1b, xor(s, a0, x0, a2), y1)

    def relay_source(t):
        return at(core, y0, a2, a1, a0, zh, x1b, t, xor(y1, a1))

    def final_of(t):
        return at(zh, x1b, t, xor(y1, a1), xor(x0, a0, t, a2), core, y0, a2, a1)

    def final_source(s):
        return at(xor(a1, core), x1b, x0, core, s, y1, y0, xor(a0, s, a2, x0), zh)

    def block_of(ph):
        return xor(a0, ph)

    def slot_of(ph):
        return xor(x0, a2, ph)

    has_below = row > 0
    has_above = row < 31
    below = (jnp.maximum(row - 1, 0), col)
    above = (jnp.minimum(row + 1, 31), col)

    barrier = pltpu.get_barrier_semaphore()

    def greet(device, on):
        @pl.when(on)
        def _():
            pl.semaphore_signal(barrier, inc=1, device_id=device, device_id_type=MESH)

    greet(below, has_below)
    greet(above, has_above)
    count = has_below.astype(jnp.int32) + has_above.astype(jnp.int32)
    for s in range(2):
        for device in (relay_source(s), final_source(s)):
            greet(device, other(device))
        for device in (relay_of(s), final_of(s)):
            count = count + other(device).astype(jnp.int32)

    for ta in range(NT):
        for tb in range(NT):
            rows, cols = pl.ds(ta * TILE, TILE), pl.ds(tb * TILE, TILE)
            fe[rows, cols] = fock_ref[rows, cols] * ftile_ref[ta, tb].astype(jnp.float32)
            se[rows, cols] = over_ref[rows, cols] * otile_ref[ta, tb].astype(jnp.float32)

    pl.semaphore_wait(barrier, count)

    def rows_of(c):
        return pl.ds(c * CH, CH)

    def halo_copies(it, s, c):
        source = x_ref.at[0, s, rows_of(c)] if it == 0 else x1.at[s, rows_of(c)]
        copies = []
        for way, device in ((0, above), (1, below)):
            n = ((it * 2 + way) * 2 + s) * NCH + c
            copies.append(pltpu.make_async_remote_copy(
                src_ref=source, dst_ref=hbuf.at[it, way, s, rows_of(c)], send_sem=hs.at[n], recv_sem=hr.at[n],
                device_id=device, device_id_type=MESH))
        return copies

    def halo_start(it, s, c):
        up, down = halo_copies(it, s, c)

        @pl.when(has_above)
        def _():
            up.start()

        @pl.when(has_below)
        def _():
            down.start()

    def halo_wait_send(it, s, c):
        up, down = halo_copies(it, s, c)

        @pl.when(has_above)
        def _():
            up.wait_send()

        @pl.when(has_below)
        def _():
            down.wait_send()

    def halo_wait_recv(it, s, c):
        up, down = halo_copies(it, s, c)

        @pl.when(has_below)
        def _():
            up.wait_recv()

        @pl.when(has_above)
        def _():
            down.wait_recv()

    def leg(source, target, send, recv, device):
        def remote():
            return pltpu.make_async_remote_copy(
                src_ref=source, dst_ref=target, send_sem=send, recv_sem=recv, device_id=device, device_id_type=MESH)

        def local():
            return pltpu.make_async_copy(source, target, recv)

        return remote, local

    def leg1(it, s, c):
        device = relay_of(s)
        return leg(
            gt.at[it, s, rows_of(c)], rbuf.at[it, x0, rows_of(c)],
            l1s.at[(it * 2 + s) * NCH + c], l1r.at[(it * 2 + x0) * NCH + c], device), other(device)

    def leg2(it, t, c):
        device = final_of(t)
        return leg(
            rbuf.at[it, t, rows_of(c)], mbuf.at[it, a0, rows_of(c)],
            l2s.at[(it * 2 + t) * NCH + c], l2r.at[(it * 2 + a0) * NCH + c], device), other(device)

    def leg_start(pair):
        (remote, local), on = pair

        @pl.when(on)
        def _():
            remote().start()

        @pl.when(jnp.logical_not(on))
        def _():
            local().start()

    def leg_wait_send(pair):
        (remote, _), on = pair

        @pl.when(on)
        def _():
            remote().wait_send()

    def landed(buffer, semaphore):
        pltpu.make_async_copy(buffer, buffer, semaphore).wait()

    for s in range(2):
        for it in range(ITERS):
            @pl.when(jnp.logical_not(has_below))
            def _():
                hbuf[it, 0, s] = jnp.zeros((NV, NV), jnp.float32)

            @pl.when(jnp.logical_not(has_above))
            def _():
                hbuf[it, 1, s] = jnp.zeros((NV, NV), jnp.float32)

    b0, b1 = block_of(0), block_of(1)
    for c in range(NCH):
        halo_start(0, b1, c)
    for c in range(NCH):
        halo_start(0, b0, c)

    prev, succ = jnp.maximum(row - 1, 0), jnp.minimum(row + 1, 31)
    c_own = occ_ref[row, row] * opat_ref[row, row].astype(jnp.float32)
    c_below = occ_ref[row, prev] * opat_ref[row, prev].astype(jnp.float32) * has_below.astype(jnp.float32)
    c_above = occ_ref[row, succ] * opat_ref[row, succ].astype(jnp.float32) * has_above.astype(jnp.float32)
    mm[...] = fe[...] - c_own * se[...]

    def own_part(it, s):
        current = x_ref[0, s] if it == 0 else x1[s]
        dd[s] = dot_nn(dot_nt(se[...], current), mm[...])

    def half_residual(it, s):
        for c in range(NCH):
            halo_wait_recv(it, s, c)
            near = c_below * hbuf[it, 0, s, rows_of(c)] + c_above * hbuf[it, 1, s, rows_of(c)]
            vtw[:, rows_of(c)] = dot_nt(se[...], near)
        for c in range(NCH):
            gt[it, s, rows_of(c)] = dd[s, rows_of(c)] - dot_nn(vtw[rows_of(c)], se[...])
            leg_start(leg1(it, s, c))
        gg[s] = jnp.transpose(gt[it, s])

    def forward(it, t):
        for c in range(NCH):
            landed(rbuf.at[it, t, rows_of(c)], l1r.at[(it * 2 + t) * NCH + c])
            leg_start(leg2(it, t, c))

    def make_scale(s):
        pair = 2 * col + s
        shift = occ_ref[row, row] + occ_ref[pair, pair]
        for ta in range(NT):
            for tb in range(NT):
                rows, cols = pl.ds(ta * TILE, TILE), pl.ds(tb * TILE, TILE)
                both = (dom_ref[0, s, ta] * dom_ref[0, s, tb]).astype(jnp.float32)
                scale[s, rows, cols] = both / (ener[rows, cols] - shift)

    def update(it, s):
        for c in range(NCH):
            rows = rows_of(c)
            landed(mbuf.at[it, s, rows], l2r.at[(it * 2 + s) * NCH + c])
            residual = k_ref[0, s, rows] + gg[s, rows] + mbuf[it, s, rows]
            if it == 0:
                x1[s, rows] = x_ref[0, s, rows] - scale[s, rows] * residual
                halo_start(1, s, c)
            else:
                out_ref[0, s, rows] = x1[s, rows] - scale[s, rows] * residual

    across = jnp.broadcast_to(ener_ref[...], (NV, NV))
    own_part(0, b0)
    ener[...] = across + jnp.transpose(across)
    make_scale(b0)
    make_scale(b1)
    half_residual(0, b0)
    own_part(0, b1)
    forward(0, slot_of(0))
    half_residual(0, b1)
    forward(0, slot_of(1))
    update(0, b0)
    own_part(1, b0)
    update(0, b1)
    own_part(1, b1)
    half_residual(1, b1)
    forward(1, slot_of(1))
    half_residual(1, b0)
    forward(1, slot_of(0))
    update(1, b1)
    update(1, b0)
    for it in range(ITERS):
        for s in range(2):
            for c in range(NCH):
                halo_wait_send(it, s, c)
                leg_wait_send(leg1(it, s, c))
                leg_wait_send(leg2(it, s, c))


def shards(
    amplitudes, exchange_ints, virt_fock, intersection, occ_fock, virt_energy, fock_tiles, intersection_tiles,
    occ_pattern, pair_domain,
):
    vmem, smem = pl.BlockSpec(memory_space=pltpu.VMEM), pl.BlockSpec(memory_space=pltpu.SMEM)
    block = (NV, NV)
    return pl.pallas_call(
        kernel,
        out_shape=jax.ShapeDtypeStruct(amplitudes.shape, jnp.float32),
        in_specs=[vmem, vmem, vmem, vmem, smem, vmem, smem, smem, smem, smem],
        out_specs=vmem,
        scratch_shapes=[
            pltpu.VMEM(block, jnp.float32),
            pltpu.VMEM(block, jnp.float32),
            pltpu.VMEM(block, jnp.float32),
            pltpu.VMEM((2,) + block, jnp.float32),
            pltpu.VMEM((ITERS, 2, 2) + block, jnp.float32),
            pltpu.VMEM((ITERS, 2) + block, jnp.float32),
            pltpu.VMEM((ITERS, 2) + block, jnp.float32),
            pltpu.VMEM((ITERS, 2) + block, jnp.float32),
            pltpu.VMEM((2,) + block, jnp.float32),
            pltpu.VMEM((2,) + block, jnp.float32),
            pltpu.VMEM((2,) + block, jnp.float32),
            pltpu.VMEM(block, jnp.float32),
            pltpu.VMEM(block, jnp.float32),
            pltpu.SemaphoreType.DMA((ITERS * 2 * 2 * NCH,)),
            pltpu.SemaphoreType.DMA((ITERS * 2 * 2 * NCH,)),
            pltpu.SemaphoreType.DMA((ITERS * 2 * NCH,)),
            pltpu.SemaphoreType.DMA((ITERS * 2 * NCH,)),
            pltpu.SemaphoreType.DMA((ITERS * 2 * NCH,)),
            pltpu.SemaphoreType.DMA((ITERS * 2 * NCH,)),
        ],
        compiler_params=pltpu.CompilerParams(collective_id=0, has_side_effects=True, vmem_limit_bytes=48 * 1024 * 1024),
        cost_estimate=pl.CostEstimate(flops=32 * NV * NV * NV, bytes_accessed=24 * NV * NV, transcendentals=0),
    )(
        amplitudes, exchange_ints, virt_fock, intersection, occ_fock, virt_energy.reshape(1, NV), fock_tiles,
        intersection_tiles, occ_pattern, pair_domain,
    )


def solution(mesh):
    in_specs = (
        P("row", "col", None, None),
        P("row", "col", None, None),
        P(),
        P(),
        P(),
        P(),
        P(),
        P(),
        P(),
        P("row", "col", None),
    )
    out_specs = P("row", "col", None, None)
    return jax.shard_map(shards, mesh=mesh, in_specs=in_specs, out_specs=out_specs, check_vma=False)
```

time: 580 us -> 250 us (0.43)
  the two profiles are of different devices: /device:TPU:33 before, /device:TPU:15 now
where the time goes in v1:
time: 250 us; the launch traced here: 249 us
  Pallas kernels  239 us (96%)
  local copies, waits for them, and re-layouts  9.84 us (4%)
    pallas_call x1, Pallas kernels, shards(): pl.pallas_call(kernel, out_shape=jax.ShapeDtypeStruct(amplitudes.shape, j...  239 us
    unnamed x19, local copies, waits for them, and re-layouts  9.16 us

profile of v1, /device:TPU:15, one launch (start us, length us, event | category | flops | bytes accessed | tf_op | source)
XLA Modules:
  0.0 249.1 jit_solution(12567618534896133595)
XLA Ops:
  0.0 0.7 reshape.3.ener_ref
  0.7 0.0 copy-start
  0.7 1.3 copy-done
  2.0 0.0 copy-start.1
  2.0 1.3 copy-done.1
  3.2 0.0 copy-start.2
  3.2 1.1 copy-done.2
  4.3 0.0 copy-start.3
  4.3 1.1 copy-done.3
  5.4 0.0 copy-start.4
  5.4 0.7 copy-done.4
  6.1 0.0 copy-start.5
  6.1 0.7 copy-done.5
  6.8 0.0 copy-start.6
  6.8 0.7 copy-done.6
  7.5 0.0 copy-start.7
  7.5 0.7 copy-done.7
  8.2 0.0 copy-start.8
  8.2 0.7 copy-done.8
  8.8 239.2 %shard_map.100 = f32[1,2,384,384]{3,2,1,0:T(8,128)S(1)} custom-call(f32[1,2,384,384]{3,2,1,0:T(8,128)S(1)} %copy-done, f32[1,2,384,384]{3,2,1,0:T(8,128)S(1)} %copy-done.1, f32[384,384]{1,0:T(8,128)S(1)} %copy-done.2, f32[384,384]{1,0:T(8,128)S(1)} %copy-done.3, f32[32,32]{1,0:T(8,128)S(1)} %copy-done.4, f32[1,384]{1,0:T(1,128)S(1)} %reshape.3.ener_ref, ...), custom_call_target="tpu_custom_call" | custom-call | flops 1811939328 | bytes 3538944 | tf_op jit(solution)/shard_map/pallas_call | solution.py:287
  248.1 1.0 copy.12
Async XLA Ops:
  0.7 1.3 copy-start
  2.0 1.3 copy-start.1
  3.2 1.1 copy-start.2
  4.3 1.1 copy-start.3
  5.4 0.7 copy-start.4
  6.1 0.7 copy-start.5
  6.8 0.7 copy-start.6
  7.5 0.7 copy-start.7
  8.2 0.7 copy-start.8

commit v2 on v0

v2 whole, which is shorter than its diff:
```python
import jax
import jax.numpy as jnp
from jax import lax
from jax.experimental import pallas as pl
from jax.experimental.pallas import tpu as pltpu
from jax.sharding import PartitionSpec as P

TILE = 128
NT = 3
NV = 384
NCH = 3
CH = NV // NCH
ITERS = 2
HEAD = 8
MESH = pl.DeviceIdType.MESH
HIGHEST = lax.Precision.HIGHEST


def bit(value, place):
    return (value // (1 << place)) % 2


def xor(left, right):
    return (left + right) % 2


def xor3(left, right):
    return sum(xor(bit(left, n), bit(right, n)) * (1 << n) for n in range(3))


def less(left, right):
    return (right - left + 7) // 8


def pick(flag, yes, no):
    return flag * yes + (1 - flag) * no


def parts(index):
    return index // 16, bit(index, 3), index % 8


def is_first(i, j):
    p, u, a = parts(i)
    q, v, b = parts(j)
    near = xor(less(b, a), 1 - u)
    return pick(xor(u, v), u, pick(xor(p, q), xor(p, u), near))


def spot(i, j, zh, zl):
    p, u, a = parts(i)
    q, v, b = parts(j)
    m = xor3(a, b)
    return (2 * xor(u, v) + m // 4) * 8 + zl, zh * 8 + (m % 4) * 2 + xor(p, q)


def manager(i, j):
    first = is_first(i, j)
    zh = pick(first, j // 16, i // 16)
    zl = pick(first, i % 8, j % 8)
    return spot(i, j, zh, zl), 1 - first


def in_plane(i, j):
    return spot(i, j, j // 16, i % 8), 1 - is_first(i, j)


def held(row, col):
    y, a, q = row // 8, row % 8, col // 8
    c, d = y // 2, col % 2
    m = 4 * (y % 2) + (col // 2) % 4
    b = xor3(a, m)
    p = xor(q, d)
    diag = (1 - c) * (1 - d) * ((7 - m) // 7)
    same = pick(d, q, less(b, a))
    u = pick(c, 1, same)
    v = (1 - c) * (same + diag)
    one, two = 16 * p + 8 * u + a, 16 * q + 8 * v + b
    partner = y * 8 + b, p * 8 + col % 8
    return (one, pick(diag, one, two)), (two, pick(diag, two, one)), diag, partner


def home(i, j):
    return i, j // 2


def dot_nt(left, right):
    return lax.dot_general(left, right, (((1,), (1,)), ((), ())), precision=HIGHEST, preferred_element_type=jnp.float32)


def dot_nn(left, right):
    return lax.dot_general(left, right, (((1,), (0,)), ((), ())), precision=HIGHEST, preferred_element_type=jnp.float32)


def rows_of(c):
    return pl.ds(c * CH, CH)


def e_rows_of(c):
    return pl.ds(0, CH + HEAD) if c == 0 else pl.ds(HEAD + c * CH, CH)


def tile_of(t):
    return pl.ds(t * TILE, TILE)


def kernel(
    x_ref, k_ref, fock_ref, over_ref, occ_ref, ener_ref, ftile_ref, otile_ref, opat_ref, dom_ref,
    out_ref,
    fe, se, mm, ener, xin, ein, e0, scale, rden, x1, hbuf, gt, dd, vtw, hsum, hout, hin,
    xs, xr, es, er, xs2, xr2, es2, er2, hs, hr, os, orc,
):
    row = lax.axis_index("row")
    col = lax.axis_index("col")

    def other(device):
        return jnp.logical_or(device[0] != row, device[1] != col)

    own = [(row, 2 * col + s) for s in range(2)]
    first_hop = [in_plane(*pair) for pair in own]
    managed_at = [manager(*pair) for pair in own]
    one, two, diag, partner = held(row, col)
    blocks = (one, two)
    relayed = held(*partner)[1]
    targets = []
    for k, l in blocks:
        ways = []
        for step in (1, -1):
            there = jnp.logical_and(k + step >= 0, k + step <= 31)
            device, w = manager(jnp.clip(k + step, 0, 31), l)
            ways.append((device, w, there))
        targets.append(ways)

    barrier = pltpu.get_barrier_semaphore()

    def greet(device, on):
        @pl.when(on)
        def _():
            pl.semaphore_signal(barrier, inc=1, device_id=device, device_id_type=MESH)

    count = jnp.int32(0)
    for device in (home(*one), home(*relayed), partner, managed_at[0][0], managed_at[1][0]):
        greet(device, other(device))
    for device in (first_hop[0][0], first_hop[1][0], partner, home(*one), home(*two)):
        count = count + other(device).astype(jnp.int32)
    for ways in targets:
        for device, _, there in ways:
            greet(device, there)
            count = count + there.astype(jnp.int32)

    for w in range(2):
        for way in range(2):
            @pl.when(jnp.logical_not(targets[w][1 - way][2]))
            def _():
                for it in range(ITERS):
                    hbuf[it, way, w] = jnp.zeros((NV, NV), jnp.float32)

    pl.semaphore_wait(barrier, count)

    def remote(source, target, send, recv, device):
        return pltpu.make_async_remote_copy(
            src_ref=source, dst_ref=target, send_sem=send, recv_sem=recv, device_id=device, device_id_type=MESH)

    def start(args, device):
        @pl.when(other(device))
        def _():
            remote(*args, device).start()

        @pl.when(jnp.logical_not(other(device)))
        def _():
            pltpu.make_async_copy(args[0], args[1], args[3]).start()

    def wait_send(args, device):
        @pl.when(other(device))
        def _():
            remote(*args, device).wait_send()

    def landed(buffer, semaphore):
        pltpu.make_async_copy(buffer, buffer, semaphore).wait()

    def x_hop(s, c):
        device, w = first_hop[s]
        return (x_ref.at[0, s, rows_of(c)], xin.at[2 * w, rows_of(c)], xs.at[s * NCH + c], xr.at[w * NCH + c]), device

    def e_hop(s, c):
        device, w = first_hop[s]
        return (e0.at[s, e_rows_of(c)], ein.at[2 * w, e_rows_of(c)], es.at[s * NCH + c], er.at[w * NCH + c]), device

    def x_relay(c):
        return (xin.at[2, rows_of(c)], xin.at[1, rows_of(c)], xs2.at[c], xr2.at[c]), partner

    def e_relay(c):
        return (ein.at[2, e_rows_of(c)], ein.at[1, e_rows_of(c)], es2.at[c], er2.at[c]), partner

    def x_landed(w, c):
        landed(xin.at[w, rows_of(c)], xr2.at[c] if w else xr.at[c])

    def e_landed(w, c):
        landed(ein.at[w, e_rows_of(c)], er2.at[c] if w else er.at[c])

    def halo(it, w, way, c):
        device, there_w, _ = targets[w][way]
        source = xin.at[w, rows_of(c)] if it == 0 else x1.at[w, rows_of(c)]
        return (
            source, hbuf.at[it, way, there_w, rows_of(c)], hs.at[((it * 2 + way) * 2 + w) * NCH + c],
            hr.at[((it * 2 + way) * 2 + there_w) * NCH + c], device)

    def halo_start(it, w, c):
        for way in range(2):
            @pl.when(targets[w][way][2])
            def _():
                remote(*halo(it, w, way, c)).start()

    def halo_wait_send(it, w, c):
        for way in range(2):
            @pl.when(targets[w][way][2])
            def _():
                remote(*halo(it, w, way, c)).wait_send()

    def halo_landed(it, w, c):
        for way in range(2):
            @pl.when(targets[w][1 - way][2])
            def _():
                landed(hbuf.at[it, way, w, rows_of(c)], hr.at[((it * 2 + way) * 2 + w) * NCH + c])

    def back(w, c):
        slot = blocks[w][1] % 2
        return (
            hout.at[w, rows_of(c)], hin.at[slot, rows_of(c)], os.at[w * NCH + c], orc.at[slot * NCH + c]), home(*blocks[w])

    for c in range(NCH):
        for s in range(2):
            start(*x_hop(s, c))

    for ta in range(NT):
        for tb in range(NT):
            rows, cols = tile_of(ta), tile_of(tb)
            fe[rows, cols] = fock_ref[rows, cols] * ftile_ref[ta, tb].astype(jnp.float32)
            se[rows, cols] = over_ref[rows, cols] * otile_ref[ta, tb].astype(jnp.float32)
    across = jnp.broadcast_to(ener_ref[...], (NV, NV))
    ener[...] = across + jnp.transpose(across)

    def at_home(s):
        i, j = own[s]
        shift = occ_ref[i, i] + occ_ref[j, j]
        for ta in range(NT):
            e0[s, pl.ds(0, HEAD), tile_of(ta)] = jnp.full((HEAD, TILE), dom_ref[0, s, ta].astype(jnp.float32))
            for tb in range(NT):
                rows, cols = tile_of(ta), tile_of(tb)
                both = (dom_ref[0, s, ta] * dom_ref[0, s, tb]).astype(jnp.float32)
                scale[s, rows, cols] = both / (ener[rows, cols] - shift)
        e0[s, pl.ds(HEAD, NV)] = x_ref[0, s] - scale[s] * k_ref[0, s]

    at_home(0)
    for c in range(NCH):
        landed(xin.at[2, rows_of(c)], xr.at[NCH + c])
        start(*x_relay(c))
    at_home(1)
    for c in range(NCH):
        for s in range(2):
            start(*e_hop(s, c))
    for c in range(NCH):
        x_landed(0, c)
        halo_start(0, 0, c)

    factors = []
    for w, (k, l) in enumerate(blocks):
        lower, upper = jnp.maximum(k - 1, 0), jnp.minimum(k + 1, 31)
        c_own = occ_ref[k, k] * opat_ref[k, k].astype(jnp.float32)
        c_below = occ_ref[k, lower] * opat_ref[k, lower].astype(jnp.float32)
        c_above = occ_ref[k, upper] * opat_ref[k, upper].astype(jnp.float32)
        factors.append((
            c_below * targets[w][1][2].astype(jnp.float32),
            c_above * targets[w][0][2].astype(jnp.float32)))
        mm[w] = fe[...] - c_own * se[...]
        rden[w] = 1.0 / (ener[...] - (occ_ref[k, k] + occ_ref[l, l]))

    def own_part(it, w):
        current = xin[w] if it == 0 else x1[w]
        dd[w] = dot_nn(dot_nt(se[...], current), mm[w])

    def half_residual(it, w):
        c_below, c_above = factors[w]
        for c in range(NCH):
            halo_landed(it, w, c)
            near = c_below * hbuf[it, 0, w, rows_of(c)] + c_above * hbuf[it, 1, w, rows_of(c)]
            vtw[:, rows_of(c)] = dot_nt(se[...], near)
        gt[w] = dd[w] - dot_nn(vtw[...], se[...])

    sources = (pick(diag, 0, 1), pick(diag, 1, 0))

    def both_halves(w, c):
        return jnp.transpose(gt[w, :, rows_of(c)]) + gt[sources[w], rows_of(c)]

    own_part(0, 0)
    for c in range(NCH):
        x_landed(1, c)
        halo_start(0, 1, c)
        landed(ein.at[2, e_rows_of(c)], er.at[NCH + c])
        start(*e_relay(c))
    own_part(0, 1)
    half_residual(0, 0)
    half_residual(0, 1)
    for c in range(NCH):
        for w in range(2):
            e_landed(w, c)
            total = both_halves(w, c)
            hsum[w, rows_of(c)] = total
            for t in range(NT):
                mask = ein[w, pl.ds(0, 1), tile_of(c)] * ein[w, pl.ds(0, 1), tile_of(t)]
                step = mask * rden[w, rows_of(c), tile_of(t)]
                x1[w, rows_of(c), tile_of(t)] = (
                    ein[w, pl.ds(HEAD + c * CH, CH), tile_of(t)] - step * total[:, t * TILE:(t + 1) * TILE])
            halo_start(1, w, c)
    own_part(1, 0)
    own_part(1, 1)
    half_residual(1, 0)
    half_residual(1, 1)
    for c in range(NCH):
        for w in (1, 0):
            hout[w, rows_of(c)] = hsum[w, rows_of(c)] + both_halves(w, c)
            start(*back(w, c))
    for c in range(NCH):
        for s in range(2):
            rows = rows_of(c)
            landed(hin.at[s, rows], orc.at[s * NCH + c])
            out_ref[0, s, rows] = e0[s, pl.ds(HEAD + c * CH, CH)] - scale[s, rows] * (k_ref[0, s, rows] + hin[s, rows])
    for c in range(NCH):
        for s in range(2):
            wait_send(*x_hop(s, c))
            wait_send(*e_hop(s, c))
            wait_send(*back(s, c))
            for it in range(ITERS):
                halo_wait_send(it, s, c)
        wait_send(*x_relay(c))
        wait_send(*e_relay(c))


def shards(
    amplitudes, exchange_ints, virt_fock, intersection, occ_fock, virt_energy, fock_tiles, intersection_tiles,
    occ_pattern, pair_domain,
):
    vmem, smem = pl.BlockSpec(memory_space=pltpu.VMEM), pl.BlockSpec(memory_space=pltpu.SMEM)

    def room(*lead, rows=NV):
        return pltpu.VMEM(lead + (rows, NV), jnp.float32)

    def semaphores(n):
        return pltpu.SemaphoreType.DMA((n * NCH,))

    return pl.pallas_call(
        kernel,
        out_shape=jax.ShapeDtypeStruct(amplitudes.shape, jnp.float32),
        in_specs=[vmem, vmem, vmem, vmem, smem, vmem, smem, smem, smem, smem],
        out_specs=vmem,
        scratch_shapes=[
            room(), room(), room(2), room(),
            room(3), room(3, rows=NV + HEAD), room(2, rows=NV + HEAD),
            room(2), room(2), room(2),
            room(ITERS, 2, 2), room(2), room(2), room(),
            room(2), room(2), room(2),
            semaphores(2), semaphores(2), semaphores(2), semaphores(2),
            semaphores(1), semaphores(1), semaphores(1), semaphores(1),
            semaphores(4 * ITERS), semaphores(4 * ITERS), semaphores(2), semaphores(2),
        ],
        compiler_params=pltpu.CompilerParams(collective_id=0, has_side_effects=True, vmem_limit_bytes=52 * 1024 * 1024),
        cost_estimate=pl.CostEstimate(flops=32 * NV * NV * NV, bytes_accessed=24 * NV * NV, transcendentals=0),
    )(
        amplitudes, exchange_ints, virt_fock, intersection, occ_fock, virt_energy.reshape(1, NV), fock_tiles,
        intersection_tiles, occ_pattern, pair_domain,
    )


def solution(mesh):
    in_specs = (
        P("row", "col", None, None),
        P("row", "col", None, None),
        P(),
        P(),
        P(),
        P(),
        P(),
        P(),
        P(),
        P("row", "col", None),
    )
    out_specs = P("row", "col", None, None)
    return jax.shard_map(shards, mesh=mesh, in_specs=in_specs, out_specs=out_specs, check_vma=False)
```

time: 580 us -> 203 us (0.35)
  the two profiles are of different devices: /device:TPU:33 before, /device:TPU:28 now
where the time goes in v2:
time: 203 us
  Pallas kernels  194 us (96%)
  local copies, waits for them, and re-layouts  8.64 us (4%)
    pallas_call x1, Pallas kernels, shards(): pl.pallas_call(kernel, out_shape=jax.ShapeDtypeStruct(amplitudes.shape, j...  194 us
    unnamed x15, local copies, waits for them, and re-layouts  7.96 us

profile of v2, /device:TPU:28, one launch (start us, length us, event | category | flops | bytes accessed | tf_op | source)
XLA Modules:
  0.0 202.6 jit_solution(8836861917244364658)
XLA Ops:
  0.0 0.7 reshape.3.ener_ref
  0.7 0.0 copy-start
  0.7 1.1 copy-done
  1.7 0.0 copy-start.1
  1.8 1.1 copy-done.1
  2.8 0.0 copy-start.2
  2.8 0.7 copy-done.2
  3.5 0.0 copy-start.3
  3.5 0.7 copy-done.3
  4.2 0.0 copy-start.4
  4.3 0.7 copy-done.4
  4.9 0.0 copy-start.5
  4.9 0.7 copy-done.5
  5.6 0.0 copy-start.6
  5.6 0.7 copy-done.6
  6.3 194.0 %shard_map.100 = f32[1,2,384,384]{3,2,1,0:T(8,128)} custom-call(f32[1,2,384,384]{3,2,1,0:T(8,128)} %x_ref.1, f32[1,2,384,384]{3,2,1,0:T(8,128)} %k_ref.1, f32[384,384]{1,0:T(8,128)S(1)} %copy-done, f32[384,384]{1,0:T(8,128)S(1)} %copy-done.1, f32[32,32]{1,0:T(8,128)S(1)} %copy-done.2, f32[1,384]{1,0:T(1,128)S(1)} %reshape.3.ener_ref, s32[3,3]{1,0:T(4,128)S(1)} %copy-done.4, ...), custom_call_target="tpu_custom_call" | custom-call | flops 1811939328 | bytes 3538944 | tf_op jit(solution)/shard_map/pallas_call | solution.py:351
  200.3 2.4 %copy.12 = f32[1,2,384,384]{3,2,1,0:T(8,128)} copy(f32[1,2,384,384]{3,2,1,0:T(8,128)} %shard_map.100) | data formatting | bytes 2359296
Async XLA Ops:
  0.7 1.1 copy-start
  1.7 1.1 copy-start.1
  2.8 0.7 copy-start.2
  3.5 0.7 copy-start.3
  4.2 0.7 copy-start.4
  4.9 0.7 copy-start.5
  5.6 0.7 copy-start.6

commit v3 on v2

--- a/solution.py
+++ b/solution.py
@@ -105,10 +105,11 @@
 
 
 def kernel(
+    x_hbm, k_hbm, fock_hbm, over_hbm, occ_hbm, ener_hbm, ftile_hbm, otile_hbm, opat_hbm, dom_hbm,
+    hin, scale_hbm, rest_hbm,
     x_ref, k_ref, fock_ref, over_ref, occ_ref, ener_ref, ftile_ref, otile_ref, opat_ref, dom_ref,
-    out_ref,
-    fe, se, mm, ener, xin, ein, e0, scale, rden, x1, hbuf, gt, dd, vtw, hsum, hout, hin,
-    xs, xr, es, er, xs2, xr2, es2, er2, hs, hr, os, orc,
+    fe, se, mm, ener, xin, ein, e0, scale, rest, rden, x1, hbuf, dd, hsum, hout,
+    xs, xr, es, er, xs2, xr2, es2, er2, hs, hr, os, orc, ins, outs,
 ):
     row = lax.axis_index("row")
     col = lax.axis_index("col")
@@ -116,7 +117,16 @@
     def other(device):
         return jnp.logical_or(device[0] != row, device[1] != col)
 
-    own = [(row, 2 * col + s) for s in range(2)]
+    loads = [
+        pltpu.make_async_copy(source, target, ins.at[n]) for n, (source, target) in enumerate((
+            (occ_hbm, occ_ref), (opat_hbm, opat_ref), (ftile_hbm, ftile_ref), (otile_hbm, otile_ref), (dom_hbm, dom_ref),
+            (ener_hbm, ener_ref), (fock_hbm, fock_ref), (over_hbm, over_ref), (x_hbm, x_ref), (k_hbm, k_ref)))]
+    for load in loads:
+        load.start()
+
+    early = is_first(row, 2 * col)
+    slots = (early, 1 - early)
+    own = [(row, 2 * col + s) for s in slots]
     first_hop = [in_plane(*pair) for pair in own]
     managed_at = [manager(*pair) for pair in own]
     one, two, diag, partner = held(row, col)
@@ -178,13 +188,13 @@
     def landed(buffer, semaphore):
         pltpu.make_async_copy(buffer, buffer, semaphore).wait()
 
-    def x_hop(s, c):
-        device, w = first_hop[s]
-        return (x_ref.at[0, s, rows_of(c)], xin.at[2 * w, rows_of(c)], xs.at[s * NCH + c], xr.at[w * NCH + c]), device
-
-    def e_hop(s, c):
-        device, w = first_hop[s]
-        return (e0.at[s, e_rows_of(c)], ein.at[2 * w, e_rows_of(c)], es.at[s * NCH + c], er.at[w * NCH + c]), device
+    def x_hop(n, c):
+        device, w = first_hop[n]
+        return (x_hbm.at[0, slots[n], rows_of(c)], xin.at[2 * w, rows_of(c)], xs.at[n * NCH + c], xr.at[w * NCH + c]), device
+
+    def e_hop(n, c):
+        device, w = first_hop[n]
+        return (e0.at[n, e_rows_of(c)], ein.at[2 * w, e_rows_of(c)], es.at[n * NCH + c], er.at[w * NCH + c]), device
 
     def x_relay(c):
         return (xin.at[2, rows_of(c)], xin.at[1, rows_of(c)], xs2.at[c], xr2.at[c]), partner
@@ -226,11 +236,13 @@
     def back(w, c):
         slot = blocks[w][1] % 2
         return (
-            hout.at[w, rows_of(c)], hin.at[slot, rows_of(c)], os.at[w * NCH + c], orc.at[slot * NCH + c]), home(*blocks[w])
-
-    for c in range(NCH):
-        for s in range(2):
-            start(*x_hop(s, c))
+            hout.at[w, rows_of(c)], hin.at[0, slot, rows_of(c)], os.at[w * NCH + c], orc.at[slot * NCH + c]), home(*blocks[w])
+
+    for n in range(2):
+        for c in range(NCH):
+            start(*x_hop(n, c))
+    for load in loads:
+        load.wait()
 
     for ta in range(NT):
         for tb in range(NT):
@@ -240,25 +252,34 @@
     across = jnp.broadcast_to(ener_ref[...], (NV, NV))
     ener[...] = across + jnp.transpose(across)
 
-    def at_home(s):
-        i, j = own[s]
+    def at_home(n):
+        (i, j), s = own[n], slots[n]
         shift = occ_ref[i, i] + occ_ref[j, j]
         for ta in range(NT):
-            e0[s, pl.ds(0, HEAD), tile_of(ta)] = jnp.full((HEAD, TILE), dom_ref[0, s, ta].astype(jnp.float32))
+            e0[n, pl.ds(0, HEAD), tile_of(ta)] = jnp.full((HEAD, TILE), dom_ref[0, s, ta].astype(jnp.float32))
             for tb in range(NT):
                 rows, cols = tile_of(ta), tile_of(tb)
                 both = (dom_ref[0, s, ta] * dom_ref[0, s, tb]).astype(jnp.float32)
-                scale[s, rows, cols] = both / (ener[rows, cols] - shift)
-        e0[s, pl.ds(HEAD, NV)] = x_ref[0, s] - scale[s] * k_ref[0, s]
+                scale[n, rows, cols] = both / (ener[rows, cols] - shift)
+        exchange = scale[n] * k_ref[0, s]
+        once = x_ref[0, s] - exchange
+        e0[n, pl.ds(HEAD, NV)] = once
+        rest[n] = once - exchange
+
+    def keep(n):
+        return (
+            pltpu.make_async_copy(scale.at[n], scale_hbm.at[0, slots[n]], outs.at[2 * n]),
+            pltpu.make_async_copy(rest.at[n], rest_hbm.at[0, slots[n]], outs.at[2 * n + 1]))
 
     at_home(0)
     for c in range(NCH):
         landed(xin.at[2, rows_of(c)], xr.at[NCH + c])
         start(*x_relay(c))
+    for c in range(NCH):
+        start(*e_hop(0, c))
     at_home(1)
     for c in range(NCH):
-        for s in range(2):
-            start(*e_hop(s, c))
+        start(*e_hop(1, c))
     for c in range(NCH):
         x_landed(0, c)
         halo_start(0, 0, c)
@@ -279,18 +300,18 @@
         current = xin[w] if it == 0 else x1[w]
         dd[w] = dot_nn(dot_nt(se[...], current), mm[w])
 
-    def half_residual(it, w):
-        c_below, c_above = factors[w]
+    def near_part(it):
         for c in range(NCH):
-            halo_landed(it, w, c)
-            near = c_below * hbuf[it, 0, w, rows_of(c)] + c_above * hbuf[it, 1, w, rows_of(c)]
-            vtw[:, rows_of(c)] = dot_nt(se[...], near)
-        gt[w] = dd[w] - dot_nn(vtw[...], se[...])
+            for w in range(2):
+                c_below, c_above = factors[w]
+                halo_landed(it, w, c)
+                near = c_below * hbuf[it, 0, w, rows_of(c)] + c_above * hbuf[it, 1, w, rows_of(c)]
+                dd[w] = dd[w] - dot_nn(dot_nt(se[...], near), se[rows_of(c)])
 
     sources = (pick(diag, 0, 1), pick(diag, 1, 0))
 
     def both_halves(w, c):
-        return jnp.transpose(gt[w, :, rows_of(c)]) + gt[sources[w], rows_of(c)]
+        return jnp.transpose(dd[w, :, rows_of(c)]) + dd[sources[w], rows_of(c)]
 
     own_part(0, 0)
     for c in range(NCH):
@@ -299,8 +320,7 @@
         landed(ein.at[2, e_rows_of(c)], er.at[NCH + c])
         start(*e_relay(c))
     own_part(0, 1)
-    half_residual(0, 0)
-    half_residual(0, 1)
+    near_part(0)
     for c in range(NCH):
         for w in range(2):
             e_landed(w, c)
@@ -314,17 +334,20 @@
             halo_start(1, w, c)
     own_part(1, 0)
     own_part(1, 1)
-    half_residual(1, 0)
-    half_residual(1, 1)
+    for n in range(2):
+        for copy in keep(n):
+            copy.start()
+    near_part(1)
     for c in range(NCH):
         for w in (1, 0):
             hout[w, rows_of(c)] = hsum[w, rows_of(c)] + both_halves(w, c)
             start(*back(w, c))
     for c in range(NCH):
         for s in range(2):
-            rows = rows_of(c)
-            landed(hin.at[s, rows], orc.at[s * NCH + c])
-            out_ref[0, s, rows] = e0[s, pl.ds(HEAD + c * CH, CH)] - scale[s, rows] * (k_ref[0, s, rows] + hin[s, rows])
+            landed(hin.at[0, s, rows_of(c)], orc.at[s * NCH + c])
+    for n in range(2):
+        for copy in keep(n):
+            copy.wait()
     for c in range(NCH):
         for s in range(2):
             wait_send(*x_hop(s, c))
@@ -340,35 +363,40 @@
     amplitudes, exchange_ints, virt_fock, intersection, occ_fock, virt_energy, fock_tiles, intersection_tiles,
     occ_pattern, pair_domain,
 ):
-    vmem, smem = pl.BlockSpec(memory_space=pltpu.VMEM), pl.BlockSpec(memory_space=pltpu.SMEM)
-
     def room(*lead, rows=NV):
         return pltpu.VMEM(lead + (rows, NV), jnp.float32)
 
     def semaphores(n):
         return pltpu.SemaphoreType.DMA((n * NCH,))
 
-    return pl.pallas_call(
+    whole = jax.ShapeDtypeStruct(amplitudes.shape, jnp.float32)
+    later, scale, rest = pl.pallas_call(
         kernel,
-        out_shape=jax.ShapeDtypeStruct(amplitudes.shape, jnp.float32),
-        in_specs=[vmem, vmem, vmem, vmem, smem, vmem, smem, smem, smem, smem],
-        out_specs=vmem,
+        out_shape=(whole, whole, whole),
+        in_specs=[pl.BlockSpec(memory_space=pl.ANY)] * 10,
+        out_specs=(pl.BlockSpec(memory_space=pl.ANY),) * 3,
         scratch_shapes=[
+            pltpu.VMEM(amplitudes.shape, jnp.float32), pltpu.VMEM(amplitudes.shape, jnp.float32), room(), room(),
+            pltpu.SMEM(occ_fock.shape, jnp.float32), pltpu.VMEM((1, NV), jnp.float32),
+            pltpu.SMEM((NT, NT), jnp.int32), pltpu.SMEM((NT, NT), jnp.int32),
+            pltpu.SMEM(occ_pattern.shape, jnp.int32), pltpu.SMEM(pair_domain.shape, jnp.int32),
             room(), room(), room(2), room(),
             room(3), room(3, rows=NV + HEAD), room(2, rows=NV + HEAD),
-            room(2), room(2), room(2),
-            room(ITERS, 2, 2), room(2), room(2), room(),
-            room(2), room(2), room(2),
+            room(2), room(2), room(2), room(2),
+            room(ITERS, 2, 2), room(2),
+            room(2), room(2),
             semaphores(2), semaphores(2), semaphores(2), semaphores(2),
             semaphores(1), semaphores(1), semaphores(1), semaphores(1),
             semaphores(4 * ITERS), semaphores(4 * ITERS), semaphores(2), semaphores(2),
+            pltpu.SemaphoreType.DMA((10,)), pltpu.SemaphoreType.DMA((4,)),
         ],
-        compiler_params=pltpu.CompilerParams(collective_id=0, has_side_effects=True, vmem_limit_bytes=52 * 1024 * 1024),
+        compiler_params=pltpu.CompilerParams(collective_id=0, has_side_effects=True, vmem_limit_bytes=60 * 1024 * 1024),
         cost_estimate=pl.CostEstimate(flops=32 * NV * NV * NV, bytes_accessed=24 * NV * NV, transcendentals=0),
     )(
         amplitudes, exchange_ints, virt_fock, intersection, occ_fock, virt_energy.reshape(1, NV), fock_tiles,
         intersection_tiles, occ_pattern, pair_domain,
     )
+    return rest - scale * later
 
 
 def solution(mesh):

time: 203 us -> 195 us (0.961)
  local copies, waits for them, and re-layouts: 8.64 us -> 1.24 us
  other arithmetic: 0 us -> 3.15 us
  Pallas kernels: 194 us -> 191 us
    unnamed x15 -> x0, local copies, waits for them, and re-layouts: 7.96 us -> none
    pallas_call x1, Pallas kernels: 194 us -> 191 us  [shards(): pl.pallas_call(kernel, out_shape=(whole, whole, whole), in_specs=[pl.Bloc...]
    sub x0 -> x1, other arithmetic: none -> 3.15 us  [shards(): return rest - scale * later]
where the time goes in v3:
time: 195 us
  Pallas kernels  191 us (98%)
  other arithmetic  3.15 us (2%)
    pallas_call x1, Pallas kernels, shards(): pl.pallas_call(kernel, out_shape=(whole, whole, whole), in_specs=[pl.Bloc...  191 us

profile of v3, /device:TPU:28, one launch (start us, length us, event | category | flops | bytes accessed | tf_op | source)
XLA Modules:
  0.0 195.1 jit_solution(997511302845705863)
XLA Ops:
  0.0 1.2 reshape.3.ener_hbm
  1.2 190.7 %shard_map.100 = (f32[1,2,384,384]{3,2,1,0:T(8,128)}, f32[1,2,384,384]{3,2,1,0:T(8,128)}, f32[1,2,384,384]{3,2,1,0:T(8,128)}) custom-call(f32[1,2,384,384]{3,2,1,0:T(8,128)} %x_hbm.1, f32[1,2,384,384]{3,2,1,0:T(8,128)} %k_hbm.1, f32[384,384]{1,0:T(8,128)} %fock_hbm.1, f32[384,384]{1,0:T(8,128)} %over_hbm.1, f32[32,32]{1,0:T(8,128)} %occ_hbm.1, ...), custom_call_target="tpu_custom_call" | custom-call | flops 1811939328 | bytes 3538944 | tf_op jit(solution)/shard_map/pallas_call | solution.py:373
  191.9 3.2 %multiply_subtract_fusion = f32[1,2,384,384]{3,2,1,0:T(8,128)} fusion(f32[1,2,384,384]{3,2,1,0:T(8,128)} %get-tuple-element.8, f32[1,2,384,384]{3,2,1,0:T(8,128)} %get-tuple-element.9, f32[1,2,384,384]{3,2,1,0:T(8,128)} %get-tuple-element.10), kind=kLoop, calls=%fused_computation | loop fusion | flops 589824 | bytes 4718592 | tf_op jit(solution)/shard_map/sub | solution.py:399

commit v4 on v3

--- a/solution.py
+++ b/solution.py
@@ -44,7 +44,7 @@
     p, u, a = parts(i)
     q, v, b = parts(j)
     near = xor(less(b, a), 1 - u)
-    return pick(xor(u, v), u, pick(xor(p, q), xor(p, u), near))
+    return pick(xor(u, v), xor(u, (1 - p) * (1 - q)), pick(xor(p, q), xor(p, u), near))
 
 
 def spot(i, j, zh, zl):
@@ -73,8 +73,9 @@
     p = xor(q, d)
     diag = (1 - c) * (1 - d) * ((7 - m) // 7)
     same = pick(d, q, less(b, a))
-    u = pick(c, 1, same)
-    v = (1 - c) * (same + diag)
+    apart = 1 - (1 - d) * (1 - q)
+    u = pick(c, apart, same)
+    v = pick(c, 1 - apart, same + diag)
     one, two = 16 * p + 8 * u + a, 16 * q + 8 * v + b
     partner = y * 8 + b, p * 8 + col % 8
     return (one, pick(diag, one, two)), (two, pick(diag, two, one)), diag, partner
@@ -124,8 +125,7 @@
     for load in loads:
         load.start()
 
-    early = is_first(row, 2 * col)
-    slots = (early, 1 - early)
+    slots = (0, 1)
     own = [(row, 2 * col + s) for s in slots]
     first_hop = [in_plane(*pair) for pair in own]
     managed_at = [manager(*pair) for pair in own]
@@ -138,7 +138,9 @@
         for step in (1, -1):
             there = jnp.logical_and(k + step >= 0, k + step <= 31)
             device, w = manager(jnp.clip(k + step, 0, 31), l)
-            ways.append((device, w, there))
+            planes = (device[1] // 8 - col // 8) * 8 + device[0] % 8 - row % 8
+            far = (planes + 17) % 16 > 2
+            ways.append((device, w, there, far))
         targets.append(ways)
 
     barrier = pltpu.get_barrier_semaphore()
@@ -154,7 +156,7 @@
     for device in (first_hop[0][0], first_hop[1][0], partner, home(*one), home(*two)):
         count = count + other(device).astype(jnp.int32)
     for ways in targets:
-        for device, _, there in ways:
+        for device, _, there, _ in ways:
             greet(device, there)
             count = count + there.astype(jnp.int32)
 
@@ -209,15 +211,19 @@
         landed(ein.at[w, e_rows_of(c)], er2.at[c] if w else er.at[c])
 
     def halo(it, w, way, c):
-        device, there_w, _ = targets[w][way]
+        device, there_w, _, _ = targets[w][way]
         source = xin.at[w, rows_of(c)] if it == 0 else x1.at[w, rows_of(c)]
         return (
             source, hbuf.at[it, way, there_w, rows_of(c)], hs.at[((it * 2 + way) * 2 + w) * NCH + c],
             hr.at[((it * 2 + way) * 2 + there_w) * NCH + c], device)
 
-    def halo_start(it, w, c):
+    def halo_start(it, w, c, which=None):
         for way in range(2):
-            @pl.when(targets[w][way][2])
+            _, _, there, far = targets[w][way]
+            if which is not None:
+                there = jnp.logical_and(there, far if which == "far" else jnp.logical_not(far))
+
+            @pl.when(there)
             def _():
                 remote(*halo(it, w, way, c)).start()
 
@@ -238,9 +244,14 @@
         return (
             hout.at[w, rows_of(c)], hin.at[0, slot, rows_of(c)], os.at[w * NCH + c], orc.at[slot * NCH + c]), home(*blocks[w])
 
-    for n in range(2):
+    def hops(hop, kind):
         for c in range(NCH):
-            start(*x_hop(n, c))
+            for n in range(2):
+                @pl.when(first_hop[n][1] == kind)
+                def _():
+                    start(*hop(n, c))
+
+    hops(x_hop, 1)
     for load in loads:
         load.wait()
 
@@ -271,18 +282,21 @@
             pltpu.make_async_copy(scale.at[n], scale_hbm.at[0, slots[n]], outs.at[2 * n]),
             pltpu.make_async_copy(rest.at[n], rest_hbm.at[0, slots[n]], outs.at[2 * n + 1]))
 
-    at_home(0)
     for c in range(NCH):
         landed(xin.at[2, rows_of(c)], xr.at[NCH + c])
         start(*x_relay(c))
-    for c in range(NCH):
-        start(*e_hop(0, c))
+    hops(x_hop, 0)
+    at_home(0)
     at_home(1)
-    for c in range(NCH):
-        start(*e_hop(1, c))
+    hops(e_hop, 1)
     for c in range(NCH):
         x_landed(0, c)
-        halo_start(0, 0, c)
+        halo_start(0, 0, c, "far")
+    for c in range(NCH):
+        wait_send(*x_relay(c))
+    for c in range(NCH):
+        halo_start(0, 0, c, "near")
+    hops(e_hop, 0)
 
     factors = []
     for w, (k, l) in enumerate(blocks):
@@ -317,6 +331,7 @@
     for c in range(NCH):
         x_landed(1, c)
         halo_start(0, 1, c)
+    for c in range(NCH):
         landed(ein.at[2, e_rows_of(c)], er.at[NCH + c])
         start(*e_relay(c))
     own_part(0, 1)
@@ -355,7 +370,6 @@
             wait_send(*back(s, c))
             for it in range(ITERS):
                 halo_wait_send(it, s, c)
-        wait_send(*x_relay(c))
         wait_send(*e_relay(c))
 
 

time: 195 us -> 182 us (0.933)
  the two profiles are of different devices: /device:TPU:28 before, /device:TPU:111 now
where the time goes in v4:
time: 182 us; the launch traced here: 181 us
  Pallas kernels  177 us (97%)
  other arithmetic  3.15 us (2%)
    pallas_call x1, Pallas kernels, shards(): pl.pallas_call(kernel, out_shape=(whole, whole, whole), in_specs=[pl.Bloc...  177 us

profile of v4, /device:TPU:111, one launch (start us, length us, event | category | flops | bytes accessed | tf_op | source)
XLA Modules:
  0.0 181.4 jit_solution(2427395511264430354)
XLA Ops:
  0.0 1.2 reshape.3.ener_hbm
  1.2 177.0 %shard_map.100 = (f32[1,2,384,384]{3,2,1,0:T(8,128)}, f32[1,2,384,384]{3,2,1,0:T(8,128)}, f32[1,2,384,384]{3,2,1,0:T(8,128)}) custom-call(f32[1,2,384,384]{3,2,1,0:T(8,128)} %x_hbm.1, f32[1,2,384,384]{3,2,1,0:T(8,128)} %k_hbm.1, f32[384,384]{1,0:T(8,128)} %fock_hbm.1, f32[384,384]{1,0:T(8,128)} %over_hbm.1, f32[32,32]{1,0:T(8,128)} %occ_hbm.1, ...), custom_call_target="tpu_custom_call" | custom-call | flops 1811939328 | bytes 3538944 | tf_op jit(solution)/shard_map/pallas_call | solution.py:387
  178.2 3.2 %multiply_subtract_fusion = f32[1,2,384,384]{3,2,1,0:T(8,128)} fusion(f32[1,2,384,384]{3,2,1,0:T(8,128)} %get-tuple-element.8, f32[1,2,384,384]{3,2,1,0:T(8,128)} %get-tuple-element.9, f32[1,2,384,384]{3,2,1,0:T(8,128)} %get-tuple-element.10), kind=kLoop, calls=%fused_computation | loop fusion | flops 589824 | bytes 4718592 | tf_op jit(solution)/shard_map/sub | solution.py:413

commit v5 on v4

--- a/solution.py
+++ b/solution.py
@@ -12,6 +12,7 @@
 CH = NV // NCH
 ITERS = 2
 HEAD = 8
+DIRECT = (0, 1)
 MESH = pl.DeviceIdType.MESH
 HIGHEST = lax.Precision.HIGHEST
 
@@ -110,7 +111,7 @@
     hin, scale_hbm, rest_hbm,
     x_ref, k_ref, fock_ref, over_ref, occ_ref, ener_ref, ftile_ref, otile_ref, opat_ref, dom_ref,
     fe, se, mm, ener, xin, ein, e0, scale, rest, rden, x1, hbuf, dd, hsum, hout,
-    xs, xr, es, er, xs2, xr2, es2, er2, hs, hr, os, orc, ins, outs,
+    xs, xr, es, er, xs2, xr2, es2, er2, hs, hr, ds, os, orc, ins, outs,
 ):
     row = lax.axis_index("row")
     col = lax.axis_index("col")
@@ -132,8 +133,7 @@
     one, two, diag, partner = held(row, col)
     blocks = (one, two)
     relayed = held(*partner)[1]
-    targets = []
-    for k, l in blocks:
+    def both_ways(k, l):
         ways = []
         for step in (1, -1):
             there = jnp.logical_and(k + step >= 0, k + step <= 31)
@@ -141,7 +141,14 @@
             planes = (device[1] // 8 - col // 8) * 8 + device[0] % 8 - row % 8
             far = (planes + 17) % 16 > 2
             ways.append((device, w, there, far))
-        targets.append(ways)
+        return ways
+
+    targets = [both_ways(k, l) for k, l in blocks]
+    direct = []
+    for pair, (_, kind) in zip(own, first_hop):
+        direct.append([
+            (device, w, jnp.logical_and(kind == 0, jnp.logical_and(there, jnp.logical_not(far))))
+            for device, w, there, far in both_ways(*pair)])
 
     barrier = pltpu.get_barrier_semaphore()
 
@@ -155,10 +162,16 @@
         greet(device, other(device))
     for device in (first_hop[0][0], first_hop[1][0], partner, home(*one), home(*two)):
         count = count + other(device).astype(jnp.int32)
-    for ways in targets:
-        for device, _, there, _ in ways:
+    for (k, l), ways in zip(blocks, targets):
+        for (device, w, there, far), step in zip(ways, (1, -1)):
             greet(device, there)
             count = count + there.astype(jnp.int32)
+            source = home(jnp.clip(k + step, 0, 31), l)
+            sends = jnp.logical_and(w == 0, jnp.logical_and(there, jnp.logical_not(far)))
+            greet(source, jnp.logical_and(sends, other(source)))
+    for ways in direct:
+        for device, _, on in ways:
+            count = count + jnp.logical_and(on, other(device)).astype(jnp.int32)
 
     for w in range(2):
         for way in range(2):
@@ -229,9 +242,27 @@
 
     def halo_wait_send(it, w, c):
         for way in range(2):
-            @pl.when(targets[w][way][2])
+            _, _, there, far = targets[w][way]
+            if it == 0 and w == 0 and c in DIRECT:
+                there = jnp.logical_and(there, far)
+
+            @pl.when(there)
             def _():
                 remote(*halo(it, w, way, c)).wait_send()
+
+    def direct_halo(n, way, c):
+        device, there_w, _ = direct[n][way]
+        return (
+            x_hbm.at[0, n, rows_of(c)], hbuf.at[0, way, there_w, rows_of(c)], ds.at[(n * 2 + way) * NCH + c],
+            hr.at[(way * 2 + there_w) * NCH + c]), device
+
+    def each_direct(act):
+        for c in DIRECT:
+            for n in range(2):
+                for way in range(2):
+                    @pl.when(direct[n][way][2])
+                    def _():
+                        act(*direct_halo(n, way, c))
 
     def halo_landed(it, w, c):
         for way in range(2):
@@ -252,6 +283,7 @@
                     start(*hop(n, c))
 
     hops(x_hop, 1)
+    each_direct(start)
     for load in loads:
         load.wait()
 
@@ -260,7 +292,7 @@
             rows, cols = tile_of(ta), tile_of(tb)
             fe[rows, cols] = fock_ref[rows, cols] * ftile_ref[ta, tb].astype(jnp.float32)
             se[rows, cols] = over_ref[rows, cols] * otile_ref[ta, tb].astype(jnp.float32)
-    across = jnp.broadcast_to(ener_ref[...], (NV, NV))
+    across = jnp.broadcast_to(ener_ref[...][None, :], (NV, NV))
     ener[...] = across + jnp.transpose(across)
 
     def at_home(n):
@@ -295,7 +327,8 @@
     for c in range(NCH):
         wait_send(*x_relay(c))
     for c in range(NCH):
-        halo_start(0, 0, c, "near")
+        if c not in DIRECT:
+            halo_start(0, 0, c, "near")
     hops(e_hop, 0)
 
     factors = []
@@ -363,6 +396,7 @@
     for n in range(2):
         for copy in keep(n):
             copy.wait()
+    each_direct(wait_send)
     for c in range(NCH):
         for s in range(2):
             wait_send(*x_hop(s, c))
@@ -391,7 +425,7 @@
         out_specs=(pl.BlockSpec(memory_space=pl.ANY),) * 3,
         scratch_shapes=[
             pltpu.VMEM(amplitudes.shape, jnp.float32), pltpu.VMEM(amplitudes.shape, jnp.float32), room(), room(),
-            pltpu.SMEM(occ_fock.shape, jnp.float32), pltpu.VMEM((1, NV), jnp.float32),
+            pltpu.SMEM(occ_fock.shape, jnp.float32), pltpu.VMEM((NV,), jnp.float32),
             pltpu.SMEM((NT, NT), jnp.int32), pltpu.SMEM((NT, NT), jnp.int32),
             pltpu.SMEM(occ_pattern.shape, jnp.int32), pltpu.SMEM(pair_domain.shape, jnp.int32),
             room(), room(), room(2), room(),
@@ -401,13 +435,13 @@
             room(2), room(2),
             semaphores(2), semaphores(2), semaphores(2), semaphores(2),
             semaphores(1), semaphores(1), semaphores(1), semaphores(1),
-            semaphores(4 * ITERS), semaphores(4 * ITERS), semaphores(2), semaphores(2),
+            semaphores(4 * ITERS), semaphores(4 * ITERS), semaphores(4), semaphores(2), semaphores(2),
             pltpu.SemaphoreType.DMA((10,)), pltpu.SemaphoreType.DMA((4,)),
         ],
         compiler_params=pltpu.CompilerParams(collective_id=0, has_side_effects=True, vmem_limit_bytes=60 * 1024 * 1024),
         cost_estimate=pl.CostEstimate(flops=32 * NV * NV * NV, bytes_accessed=24 * NV * NV, transcendentals=0),
     )(
-        amplitudes, exchange_ints, virt_fock, intersection, occ_fock, virt_energy.reshape(1, NV), fock_tiles,
+        amplitudes, exchange_ints, virt_fock, intersection, occ_fock, virt_energy, fock_tiles,
         intersection_tiles, occ_pattern, pair_domain,
     )
     return rest - scale * later

time: 182 us -> 189 us (1.038)
  the two profiles are of different devices: /device:TPU:111 before, /device:TPU:20 now
where the time goes in v5:
time: 189 us
  Pallas kernels  186 us (98%)
  other arithmetic  3.15 us (2%)
    pallas_call x1, Pallas kernels, shards(): pl.pallas_call(kernel, out_shape=(whole, whole, whole), in_specs=[pl.Bloc...  186 us

profile of v5, /device:TPU:20, one launch (start us, length us, event | category | flops | bytes accessed | tf_op | source)
XLA Modules:
  0.0 189.1 jit_solution(8359105056378679759)
XLA Ops:
  0.0 186.0 %shard_map.100 = (f32[1,2,384,384]{3,2,1,0:T(8,128)}, f32[1,2,384,384]{3,2,1,0:T(8,128)}, f32[1,2,384,384]{3,2,1,0:T(8,128)}) custom-call(f32[1,2,384,384]{3,2,1,0:T(8,128)} %x_hbm.1, f32[1,2,384,384]{3,2,1,0:T(8,128)} %k_hbm.1, f32[384,384]{1,0:T(8,128)} %fock_hbm.1, f32[384,384]{1,0:T(8,128)} %over_hbm.1, f32[32,32]{1,0:T(8,128)} %occ_hbm.1, f32[384]{0:T(512)} %ener_hbm.1, ...), custom_call_target="tpu_custom_call" | custom-call | flops 1811939328 | bytes 3538944 | tf_op jit(solution)/shard_map/pallas_call | solution.py:421
  186.0 3.2 %multiply_subtract_fusion = f32[1,2,384,384]{3,2,1,0:T(8,128)} fusion(f32[1,2,384,384]{3,2,1,0:T(8,128)} %get-tuple-element.8, f32[1,2,384,384]{3,2,1,0:T(8,128)} %get-tuple-element.9, f32[1,2,384,384]{3,2,1,0:T(8,128)} %get-tuple-element.10), kind=kLoop, calls=%fused_computation | loop fusion | flops 589824 | bytes 4718592 | tf_op jit(solution)/shard_map/sub | solution.py:447

commit v6 on v5

--- a/solution.py
+++ b/solution.py
@@ -12,7 +12,7 @@
 CH = NV // NCH
 ITERS = 2
 HEAD = 8
-DIRECT = (0, 1)
+DIRECT = (0,)
 MESH = pl.DeviceIdType.MESH
 HIGHEST = lax.Precision.HIGHEST
 
@@ -230,11 +230,11 @@
             source, hbuf.at[it, way, there_w, rows_of(c)], hs.at[((it * 2 + way) * 2 + w) * NCH + c],
             hr.at[((it * 2 + way) * 2 + there_w) * NCH + c], device)
 
-    def halo_start(it, w, c, which=None):
+    def halo_start(it, w, c, only_far=False):
         for way in range(2):
             _, _, there, far = targets[w][way]
-            if which is not None:
-                there = jnp.logical_and(there, far if which == "far" else jnp.logical_not(far))
+            if only_far:
+                there = jnp.logical_and(there, far)
 
             @pl.when(there)
             def _():
@@ -323,13 +323,7 @@
     hops(e_hop, 1)
     for c in range(NCH):
         x_landed(0, c)
-        halo_start(0, 0, c, "far")
-    for c in range(NCH):
-        wait_send(*x_relay(c))
-    for c in range(NCH):
-        if c not in DIRECT:
-            halo_start(0, 0, c, "near")
-    hops(e_hop, 0)
+        halo_start(0, 0, c, only_far=c in DIRECT)
 
     factors = []
     for w, (k, l) in enumerate(blocks):
@@ -367,6 +361,7 @@
     for c in range(NCH):
         landed(ein.at[2, e_rows_of(c)], er.at[NCH + c])
         start(*e_relay(c))
+    hops(e_hop, 0)
     own_part(0, 1)
     near_part(0)
     for c in range(NCH):
@@ -404,6 +399,7 @@
             wait_send(*back(s, c))
             for it in range(ITERS):
                 halo_wait_send(it, s, c)
+        wait_send(*x_relay(c))
         wait_send(*e_relay(c))
 
 

time: 189 us -> 179 us (0.947)
  the two profiles are of different devices: /device:TPU:20 before, /device:TPU:28 now
where the time goes in v6:
time: 179 us
  Pallas kernels  176 us (98%)
  other arithmetic  3.15 us (2%)
    pallas_call x1, Pallas kernels, shards(): pl.pallas_call(kernel, out_shape=(whole, whole, whole), in_specs=[pl.Bloc...  176 us

profile of v6, /device:TPU:28, one launch (start us, length us, event | category | flops | bytes accessed | tf_op | source)
XLA Modules:
  0.0 178.8 jit_solution(13350386465384887513)
XLA Ops:
  0.0 175.7 %shard_map.100 = (f32[1,2,384,384]{3,2,1,0:T(8,128)}, f32[1,2,384,384]{3,2,1,0:T(8,128)}, f32[1,2,384,384]{3,2,1,0:T(8,128)}) custom-call(f32[1,2,384,384]{3,2,1,0:T(8,128)} %x_hbm.1, f32[1,2,384,384]{3,2,1,0:T(8,128)} %k_hbm.1, f32[384,384]{1,0:T(8,128)} %fock_hbm.1, f32[384,384]{1,0:T(8,128)} %over_hbm.1, f32[32,32]{1,0:T(8,128)} %occ_hbm.1, f32[384]{0:T(512)} %ener_hbm.1, ...), custom_call_target="tpu_custom_call" | custom-call | flops 1811939328 | bytes 3538944 | tf_op jit(solution)/shard_map/pallas_call | solution.py:417
  175.7 3.2 %multiply_subtract_fusion = f32[1,2,384,384]{3,2,1,0:T(8,128)} fusion(f32[1,2,384,384]{3,2,1,0:T(8,128)} %get-tuple-element.8, f32[1,2,384,384]{3,2,1,0:T(8,128)} %get-tuple-element.9, f32[1,2,384,384]{3,2,1,0:T(8,128)} %get-tuple-element.10), kind=kLoop, calls=%fused_computation | loop fusion | flops 589824 | bytes 4718592 | tf_op jit(solution)/shard_map/sub | solution.py:443
